TPU v7x, 32 devices: a whole 2x2x4 slice. The times are simulated.
32 devices in a mesh: normal: 4 (over z), span: 2 (over x), stream: 4 (over y, core).
Axes of the slice: x: 2, y: 2, z: 4, core: 2. Of those that a mesh axis runs over, the one named last changes fastest.
Arguments:
- iterate: float32 [192, 5, 2, 512], P('normal', None, 'span', 'stream'), may hold values from -6 to 6
- source: float32 [192, 5, 2, 512], P('normal', None, 'span', 'stream'), may hold values from -6 to 6
- pivot: float32 [192, 5, 5, 2, 512], P('normal', None, None, 'span', 'stream'), as said below
- lower: float32 [192, 5, 5, 2, 512], P('normal', None, None, 'span', 'stream'), as said below
- upper: float32 [192, 5, 5, 2, 512], P('normal', None, None, 'span', 'stream'), as said below
- coupling: float32 [4, 192, 5, 5, 2, 512], P(None, 'normal', None, None, 'span', 'stream'), may hold values from -0.6 to 0.6
- iblank: int32 [192, 2, 512], P('normal', 'span', 'stream'), may hold values from 0 to 2
- donor: int32 [192, 2, 512], P('normal', 'span', 'stream'), may hold values from 0 to 6143
Outputs:
- smoothed: float32 [192, 5, 2, 512], P('normal', None, 'span', 'stream')
Inputs may be any that keep to these rules, and one draw needn't show every extreme that they name: `donor`: an offset within a tile of 48 x 1 x 128 points. pivot blocks are full 5x5 blocks. lower and upper factor blocks are full 5x5 blocks; the recurrences stay bounded. upper factor blocks are full 5x5 blocks.
All inputs are finite; a program needn't handle non-finite values.
Results may differ from a plain program's by a relative error of at most 0.00018.
Values sent between devices are 32-bit elements; how exact they have to be, the bound alone decides.
A program may use at most 64 MiB of HBM per device.

v0:
```python
import functools
import jax
import jax.numpy as jnp
from jax import lax
from jax.experimental import pallas as pl
from jax.experimental.pallas import tpu as pltpu
from jax.sharding import PartitionSpec as P

SWEEPS = 2
N = 5
K = 8
LANES = 128
MESH = pl.DeviceIdType.MESH


def mat_vec(mat, vec):
    return [functools.reduce(jnp.add, [mat[c][e] * vec[e] for e in range(N)]) for c in range(N)]


def mat_mat(left, right):
    return [
        [functools.reduce(jnp.add, [left[c][e] * right[e][f] for e in range(N)]) for f in range(N)]
        for c in range(N)
    ]


def mat_map(function, *mats):
    return [[function(*(m[c][e] for m in mats)) for e in range(N)] for c in range(N)]


def vec_add(a, b):
    return [p + q for p, q in zip(a, b)]


def kernel(sizes, per_chunk, x_hbm, src_hbm, piv_hbm, low_hbm, upp_hbm, cpl_hbm, ibl_hbm, don_hbm, out_ref,
           xb, src, piv, low, upp, cpl, ibl, don, plane, edge_out, edge_in, vec_all, map_all,
           fw, gw, bw, scan_f, scan_b, excl, base, work, donated,
           load_sem, span_send, span_recv, edge_send, edge_recv, vec_send, vec_recv, map_send, map_recv):
    J = per_chunk
    n_normal, n_span, n_stream = sizes
    me, sp, st = lax.axis_index("normal"), lax.axis_index("span"), lax.axis_index("stream")
    span_targets = [lax.rem(sp + 1, n_span)] if n_span == 2 else [lax.rem(sp + 1, n_span), lax.rem(sp + n_span - 1, n_span)]
    stream_targets = [lax.rem(st + 1, n_stream)] if n_stream == 2 else [lax.rem(st + 1, n_stream), lax.rem(st + n_stream - 1, n_stream)]
    sides_span, sides_stream = len(span_targets), len(stream_targets)

    pairs = [(x_hbm, xb.at[0]), (low_hbm, low), (upp_hbm, upp), (don_hbm, don), (cpl_hbm, cpl),
             (src_hbm, src), (ibl_hbm, ibl), (piv_hbm, piv)]
    loads = [pltpu.make_async_copy(a, b, load_sem.at[i]) for i, (a, b) in enumerate(pairs)]
    for load in loads:
        load.start()
    ld_x, ld_low, ld_upp, ld_don, ld_cpl, ld_src, ld_ibl, ld_piv = loads

    barrier = pltpu.get_barrier_semaphore()
    for t in span_targets:
        pl.semaphore_signal(barrier, inc=1, device_id={"span": t}, device_id_type=MESH)
    for t in stream_targets:
        pl.semaphore_signal(barrier, inc=1, device_id={"stream": t}, device_id_type=MESH)
    for o in range(1, n_normal):
        pl.semaphore_signal(barrier, inc=1, device_id={"normal": lax.rem(me + o, n_normal)}, device_id_type=MESH)
    pl.semaphore_wait(barrier, sides_span + sides_stream + n_normal - 1)

    def span_copies(sweep, source):
        return [
            pltpu.make_async_remote_copy(
                src_ref=source, dst_ref=plane.at[sweep, i], send_sem=span_send.at[sweep, i],
                recv_sem=span_recv.at[sweep, i], device_id={"span": t}, device_id_type=MESH)
            for i, t in enumerate(span_targets)
        ]

    def edge_copies(sweep):
        return [
            pltpu.make_async_remote_copy(
                src_ref=edge_out.at[sweep], dst_ref=edge_in.at[sweep, i], send_sem=edge_send.at[sweep, i],
                recv_sem=edge_recv.at[sweep, i], device_id={"stream": t}, device_id_type=MESH)
            for i, t in enumerate(stream_targets)
        ]

    def normal_copies(ref, sends, recvs):
        out = []
        for o in range(1, n_normal):
            out.append(pltpu.make_async_remote_copy(
                src_ref=ref.at[me], dst_ref=ref.at[me], send_sem=sends.at[o - 1], recv_sem=recvs.at[o - 1],
                device_id={"normal": lax.rem(me + o, n_normal)}, device_id_type=MESH))
        return out

    def normal_arrivals(ref, sends, recvs):
        out = []
        for o in range(1, n_normal):
            came = lax.rem(me + n_normal - o, n_normal)
            out.append(pltpu.make_async_remote_copy(
                src_ref=ref.at[me], dst_ref=ref.at[came], send_sem=sends.at[o - 1], recv_sem=recvs.at[o - 1],
                device_id={"normal": lax.rem(me + o, n_normal)}, device_id_type=MESH))
        return out

    lane = lax.broadcasted_iota(jnp.int32, (K, LANES), 1)
    chunk = lax.broadcasted_iota(jnp.int32, (K, LANES), 0)

    def vec_rows(ref, j):
        return [ref[pl.ds(j * N + c, K, stride=J * N), :] for c in range(N)]

    def mat_rows(ref, j, first=0):
        return [[ref[pl.ds(first + j * N * N + c * N + e, K, stride=J * N * N), :] for e in range(N)] for c in range(N)]

    def get_mat(ref, *at):
        return [[ref[(*at, c, e)] for e in range(N)] for c in range(N)]

    def put_mat(ref, mat, *at):
        for c in range(N):
            for e in range(N):
                ref[(*at, c, e)] = mat[c][e]

    def send_edges(sweep):
        packed = jnp.zeros((K, LANES), jnp.float32)
        for j in range(J):
            rows = vec_rows(xb.at[sweep], j)
            for c in range(N):
                i = j * N + c
                packed = jnp.where(lane // 2 == i, pltpu.roll(rows[c], 2 * i + 1, 1), packed)
        edge_out[sweep] = packed
        copies = edge_copies(sweep)
        for copy in copies:
            copy.start()
        return copies

    span_now = span_copies(0, x_hbm)
    for copy in span_now:
        copy.start()
    ld_x.wait()
    edge_now = send_edges(0)
    pending = list(span_now) + list(edge_now)

    ld_low.wait()
    ld_upp.wait()

    first = mat_map(lambda a: -a, mat_rows(low, 0))
    put_mat(fw, first, 0)

    def fw_step(j, carry):
        carry = mat_mat(mat_map(lambda a: -a, mat_rows(low, j)), carry)
        put_mat(fw, carry, j)
        return carry

    last_f = lax.fori_loop(1, J, fw_step, first)
    start_b = mat_map(lambda a: -a, mat_rows(upp, J - 1))
    put_mat(bw, start_b, J - 1)
    put_mat(gw, last_f, J - 1)

    def bw_step(i, carry):
        j = J - 2 - i
        carry = mat_mat(mat_map(lambda a: -a, mat_rows(upp, j)), carry)
        put_mat(bw, carry, j)
        return carry

    def gw_step(i, carry):
        j = J - 2 - i
        moved = mat_mat(mat_rows(upp, j), carry)
        carry = mat_map(lambda a, b: a - b, get_mat(fw, j), moved)
        put_mat(gw, carry, j)
        return carry

    first_b = lax.fori_loop(0, J - 1, bw_step, start_b)
    first_g = lax.fori_loop(0, J - 1, gw_step, last_f)

    steps = (1, 2, 4)
    whole = last_f
    for level, s in enumerate(steps):
        put_mat(scan_f, mat_map(lambda a: jnp.where(chunk >= s, a, 0.0), whole), level)
        moved = mat_mat(whole, mat_map(lambda a: pltpu.roll(a, s, 0), whole))
        whole = mat_map(lambda a, b: jnp.where(chunk >= s, b, a), whole, moved)
    before = mat_map(lambda a: pltpu.roll(a, 1, 0), whole)
    before = [[jnp.where(chunk >= 1, before[c][e], 1.0 if c == e else 0.0) for e in range(N)] for c in range(N)]
    put_mat(excl, before, 0)
    for c in range(N):
        for e in range(N):
            map_all[me, pl.ds(c * N + e, 1), :] = whole[c][e][K - 1:K]
    seen = mat_mat(first_g, before)
    put_mat(excl, seen, 1)

    whole = first_b
    for level, s in enumerate(steps):
        put_mat(scan_b, mat_map(lambda a: jnp.where(chunk < K - s, a, 0.0), whole), level)
        moved = mat_mat(whole, mat_map(lambda a: pltpu.roll(a, K - s, 0), whole))
        whole = mat_map(lambda a, b: jnp.where(chunk < K - s, b, a), whole, moved)
    after = mat_map(lambda a: pltpu.roll(a, K - 1, 0), whole)
    after = [[jnp.where(chunk < K - 1, after[c][e], 1.0 if c == e else 0.0) for e in range(N)] for c in range(N)]
    put_mat(excl, after, 2)
    for c in range(N):
        for e in range(N):
            map_all[me, pl.ds(N * N + c * N + e, 1), :] = whole[c][e][0:1]
    seen = get_mat(excl, 1)
    for level, s in enumerate(steps):
        moved = mat_mat(get_mat(scan_b, level), mat_map(lambda a: pltpu.roll(a, K - s, 0), seen))
        seen = mat_map(jnp.add, seen, moved)
    for c in range(N):
        for e in range(N):
            map_all[me, pl.ds(2 * N * N + c * N + e, 1), :] = seen[c][e][0:1]
    put_mat(excl, mat_map(lambda a: jnp.where(chunk < K - 1, pltpu.roll(a, K - 1, 0), 0.0), seen), 1)
    map_now = normal_copies(map_all, map_send, map_recv)
    for copy in map_now:
        copy.start()
    pending += map_now

    for sweep in range(SWEEPS):
        here = xb.at[sweep]
        if sweep == 0:
            ld_don.wait()
        places = [don[pl.ds(j, K, stride=J), :] for j in range(J)]
        row_of = [p // LANES for p in places]
        col_of = [p % LANES for p in places]

        def gather_step(r, carry):
            out = []
            rows = [jnp.broadcast_to(here[pl.ds(r * N + c, 1), :], (K, LANES)) for c in range(N)]
            for j in range(J):
                hit = row_of[j] == r
                for c in range(N):
                    got = jnp.take_along_axis(rows[c], col_of[j], axis=1, mode="promise_in_bounds")
                    out.append(jnp.where(hit, got, carry[j * N + c]))
            return out

        got = lax.fori_loop(0, J * K, gather_step, [jnp.zeros((K, LANES), jnp.float32)] * (J * N))
        for i in range(J * N):
            donated[i] = got[i]

        if sweep == 0:
            for load in (ld_src, ld_ibl, ld_cpl):
                load.wait()
        for copy in edge_now:
            copy.wait_recv()
        left = edge_in[sweep, 0]
        right = edge_in[sweep, sides_stream - 1]
        lows, highs = [], []
        for j in range(J):
            rows = vec_rows(here, j)
            flag = ibl[pl.ds(j, K, stride=J), :]
            lows, highs = [], []
            for c in range(N):
                i = j * N + c
                lows.append(jnp.where(lane == 0, pltpu.roll(left, (LANES - 2 * i) % LANES, 1), pltpu.roll(rows[c], 1, 1)))
                highs.append(jnp.where(lane == LANES - 1, pltpu.roll(right, LANES - 2 - 2 * i, 1), pltpu.roll(rows[c], LANES - 1, 1)))
            c2 = mat_rows(cpl, j, 2 * J * K * N * N)
            c3 = mat_rows(cpl, j, 3 * J * K * N * N)
            s_rows = vec_rows(src, j)
            for c in range(N):
                acc = s_rows[c] + jnp.where(flag == 2, donated[j * N + c], 0.0)
                for e in range(N):
                    acc = acc - (c2[e][c] * lows[e] + c3[e][c] * highs[e])
                base[j * N + c] = acc

        for copy in span_now:
            copy.wait_recv()
        if sweep == 0:
            ld_piv.wait()

        def forward_step(j, state):
            c0 = mat_rows(cpl, j)
            c1 = mat_rows(cpl, j, J * K * N * N)
            flag = ibl[pl.ds(j, K, stride=J), :]
            x0 = vec_rows(plane.at[sweep, 0], j)
            rhs = []
            if sides_span == 1:
                both = mat_map(jnp.add, c0, c1)
                for c in range(N):
                    acc = functools.reduce(jnp.add, [both[e][c] * x0[e] for e in range(N)])
                    rhs.append(jnp.where(flag == 0, 0.0, base[j * N + c] - acc))
            else:
                x1 = vec_rows(plane.at[sweep, 1], j)
                for c in range(N):
                    acc = functools.reduce(jnp.add, [c0[e][c] * x0[e] + c1[e][c] * x1[e] for e in range(N)])
                    rhs.append(jnp.where(flag == 0, 0.0, base[j * N + c] - acc))
            scaled = mat_vec(mat_rows(piv, j), rhs)
            moved = mat_vec(mat_rows(low, j), state)
            state = [a - b for a, b in zip(scaled, moved)]
            for c in range(N):
                work[j * N + c] = state[c]
            return state

        zero = [jnp.zeros((K, LANES), jnp.float32)] * N
        f = lax.fori_loop(0, J, forward_step, zero)

        def backward_step(i, state):
            j = J - 1 - i
            moved = mat_vec(mat_rows(upp, j), state)
            state = [work[j * N + c] - moved[c] for c in range(N)]
            for c in range(N):
                work[j * N + c] = state[c]
            return state

        b = lax.fori_loop(0, J, backward_step, zero)
        for level, s in enumerate(steps):
            f = vec_add(f, mat_vec(get_mat(scan_f, level), [pltpu.roll(v, s, 0) for v in f]))
        y_in = [jnp.where(chunk >= 1, pltpu.roll(v, 1, 0), 0.0) for v in f]
        b = vec_add(b, mat_vec(get_mat(gw, 0), y_in))
        for level, s in enumerate(steps):
            b = vec_add(b, mat_vec(get_mat(scan_b, level), [pltpu.roll(v, K - s, 0) for v in b]))
        x_in = [jnp.where(chunk < K - 1, pltpu.roll(v, K - 1, 0), 0.0) for v in b]
        for c in range(N):
            vec_all[sweep, me, pl.ds(c, 1), :] = f[c][K - 1:K]
            vec_all[sweep, me, pl.ds(K + c, 1), :] = b[c][0:1]
        sends = normal_copies(vec_all.at[sweep], vec_send.at[sweep], vec_recv.at[sweep])
        for copy in sends:
            copy.start()
        pending += sends
        if sweep == 0:
            for copy in normal_arrivals(map_all, map_send, map_recv):
                copy.wait_recv()
        for copy in normal_arrivals(vec_all.at[sweep], vec_send.at[sweep], vec_recv.at[sweep]):
            copy.wait_recv()

        def apply_map(d, m, state):
            return functools.reduce(jnp.add, [
                map_all[d, pl.ds(m * N * N + e, N, stride=N), :] * state[e:e + 1] for e in range(N)])

        none = jnp.zeros((N, LANES), jnp.float32)
        entries, state, mine = [none], none, none
        for d in range(n_normal - 1):
            state = vec_all[sweep, d, pl.ds(0, N), :] + apply_map(d, 0, state)
            entries.append(state)
            mine = jnp.where(me == d + 1, state, mine)
        x_state, x_mine = none, none
        for d in range(n_normal - 1, 0, -1):
            x_state = (vec_all[sweep, d, pl.ds(K, N), :] + apply_map(d, 2, entries[d])) + apply_map(d, 1, x_state)
            x_mine = jnp.where(me == d - 1, x_state, x_mine)
        y_entry = [jnp.broadcast_to(mine[c:c + 1], (K, LANES)) for c in range(N)]
        x_entry = [jnp.broadcast_to(x_mine[c:c + 1], (K, LANES)) for c in range(N)]
        y_in = vec_add(y_in, mat_vec(get_mat(excl, 0), y_entry))
        x_in = vec_add(x_in, mat_vec(get_mat(excl, 1), y_entry))
        x_in = vec_add(x_in, mat_vec(get_mat(excl, 2), x_entry))

        target = out_ref if sweep == SWEEPS - 1 else xb.at[sweep + 1]

        def final_step(j, carry):
            more = vec_add(mat_vec(get_mat(gw, j), y_in), mat_vec(get_mat(bw, j), x_in))
            for c in range(N):
                target[pl.ds(j * N + c, K, stride=J * N), :] = work[j * N + c] + more[c]
            return carry

        lax.fori_loop(0, J, final_step, 0)
        if sweep < SWEEPS - 1:
            span_now = span_copies(sweep + 1, xb.at[sweep + 1])
            for copy in span_now:
                copy.start()
            edge_now = send_edges(sweep + 1)
            pending += list(span_now) + list(edge_now)

    for copy in pending:
        copy.wait_send()


def per_device(sizes, iterate, source, pivot, lower, upper, coupling, iblank, donor):
    points, comps, planes, lines = iterate.shape
    n_normal, n_span, n_stream = sizes
    J = points // K
    rows, mats = points * N, points * N * N
    sides_span, sides_stream = (1 if n_span == 2 else 2), (1 if n_stream == 2 else 2)
    f32 = jnp.float32
    peers = max(n_normal - 1, 1)
    scratch = [
        pltpu.VMEM((SWEEPS, rows, LANES), f32),
        pltpu.VMEM((rows, LANES), f32),
        pltpu.VMEM((mats, LANES), f32),
        pltpu.VMEM((mats, LANES), f32),
        pltpu.VMEM((mats, LANES), f32),
        pltpu.VMEM((4 * mats, LANES), f32),
        pltpu.VMEM((points, LANES), jnp.int32),
        pltpu.VMEM((points, LANES), jnp.int32),
        pltpu.VMEM((SWEEPS, sides_span, rows, LANES), f32),
        pltpu.VMEM((SWEEPS, K, LANES), f32),
        pltpu.VMEM((SWEEPS, sides_stream, K, LANES), f32),
        pltpu.VMEM((SWEEPS, n_normal, 2 * K, LANES), f32),
        pltpu.VMEM((n_normal, 80, LANES), f32),
        pltpu.VMEM((J, N, N, K, LANES), f32),
        pltpu.VMEM((J, N, N, K, LANES), f32),
        pltpu.VMEM((J, N, N, K, LANES), f32),
        pltpu.VMEM((3, N, N, K, LANES), f32),
        pltpu.VMEM((3, N, N, K, LANES), f32),
        pltpu.VMEM((3, N, N, K, LANES), f32),
        pltpu.VMEM((J * N, K, LANES), f32),
        pltpu.VMEM((J * N, K, LANES), f32),
        pltpu.VMEM((J * N, K, LANES), f32),
        pltpu.SemaphoreType.DMA((8,)),
        pltpu.SemaphoreType.DMA((SWEEPS, sides_span)),
        pltpu.SemaphoreType.DMA((SWEEPS, sides_span)),
        pltpu.SemaphoreType.DMA((SWEEPS, sides_stream)),
        pltpu.SemaphoreType.DMA((SWEEPS, sides_stream)),
        pltpu.SemaphoreType.DMA((SWEEPS, peers)),
        pltpu.SemaphoreType.DMA((SWEEPS, peers)),
        pltpu.SemaphoreType.DMA((peers,)),
        pltpu.SemaphoreType.DMA((peers,)),
    ]
    out = pl.pallas_call(
        functools.partial(kernel, sizes, J),
        out_shape=jax.ShapeDtypeStruct((rows, LANES), f32),
        in_specs=[pl.BlockSpec(memory_space=pl.ANY)] * 8,
        out_specs=pl.BlockSpec(memory_space=pltpu.VMEM),
        scratch_shapes=scratch,
        compiler_params=pltpu.CompilerParams(
            collective_id=0, has_side_effects=True, vmem_limit_bytes=32 * 1024 * 1024),
        cost_estimate=pl.CostEstimate(flops=12000000, bytes_accessed=5000000, transcendentals=0),
    )(
        iterate.reshape(rows, lines), source.reshape(rows, lines), pivot.reshape(mats, lines),
        lower.reshape(mats, lines), upper.reshape(mats, lines), coupling.reshape(4 * mats, lines),
        iblank.reshape(points, lines), donor.reshape(points, lines),
    )
    return out.reshape(points, comps, planes, lines)


def solution(mesh):
    placed = (
        P("normal", None, "span", "stream"),
        P("normal", None, "span", "stream"),
        P("normal", None, None, "span", "stream"),
        P("normal", None, None, "span", "stream"),
        P("normal", None, None, "span", "stream"),
        P(None, "normal", None, None, "span", "stream"),
        P("normal", "span", "stream"),
        P("normal", "span", "stream"),
    )
    sizes = tuple(mesh.shape[name] for name in ("normal", "span", "stream"))
    return jax.shard_map(
        functools.partial(per_device, sizes),
        mesh=mesh,
        in_specs=placed,
        out_specs=P("normal", None, "span", "stream"),
        check_vma=False,
    )
```

profile of v0, /device:TPU:0, one launch (start us, length us, event | category | flops | bytes accessed | tf_op | source)
XLA Modules:
  0.0 36.7 jit_solution(17812767645501888343)
XLA Ops:
  0.0 0.0 copy-start
  0.0 1.7 %copy-done = f32[4,48,5,5,1,128]{5,4,3,2,1,0:T(1,128)S(1)} copy-done((f32[4,48,5,5,1,128]{5,4,3,2,1,0:T(1,128)S(1)}, f32[4,48,5,5,1,128]{5,4,3,2,1,0:T(1,128)}, u32[]{:S(2)}) %copy-start) | copy-done | bytes 2457624
  1.7 0.0 copy-start.1
  1.7 1.1 %copy-done.1 = f32[48,5,5,1,128]{4,3,2,1,0:T(1,128)S(1)} copy-done((f32[48,5,5,1,128]{4,3,2,1,0:T(1,128)S(1)}, f32[48,5,5,1,128]{4,3,2,1,0:T(1,128)}, u32[]{:S(2)}) %copy-start.1) | copy-done | bytes 614424
  2.8 0.0 copy-start.2
  2.8 1.1 %copy-done.2 = f32[48,5,5,1,128]{4,3,2,1,0:T(1,128)S(1)} copy-done((f32[48,5,5,1,128]{4,3,2,1,0:T(1,128)S(1)}, f32[48,5,5,1,128]{4,3,2,1,0:T(1,128)}, u32[]{:S(2)}) %copy-start.2) | copy-done | bytes 614424
  3.8 0.0 copy-start.3
  3.8 1.1 %copy-done.3 = f32[48,5,5,1,128]{4,3,2,1,0:T(1,128)S(1)} copy-done((f32[48,5,5,1,128]{4,3,2,1,0:T(1,128)S(1)}, f32[48,5,5,1,128]{4,3,2,1,0:T(1,128)}, u32[]{:S(2)}) %copy-start.3) | copy-done | bytes 614424
  4.9 0.0 copy-start.4
  4.9 0.9 %copy-done.4 = f32[48,5,1,128]{3,2,1,0:T(1,128)S(1)} copy-done((f32[48,5,1,128]{3,2,1,0:T(1,128)S(1)}, f32[48,5,1,128]{3,2,1,0:T(1,128)}, u32[]{:S(2)}) %copy-start.4) | copy-done | bytes 122904
  5.8 0.0 copy-start.5
  5.8 0.9 %copy-done.5 = f32[48,5,1,128]{3,2,1,0:T(1,128)S(1)} copy-done((f32[48,5,1,128]{3,2,1,0:T(1,128)S(1)}, f32[48,5,1,128]{3,2,1,0:T(1,128)}, u32[]{:S(2)}) %copy-start.5) | copy-done | bytes 122904
  6.7 0.0 copy-start.6
  6.7 0.7 %copy-done.6 = s32[48,1,128]{2,1,0:T(1,128)S(1)} copy-done((s32[48,1,128]{2,1,0:T(1,128)S(1)}, s32[48,1,128]{2,1,0:T(1,128)}, u32[]{:S(2)}) %copy-start.6) | copy-done | bytes 24600
  7.5 0.0 copy-start.7
  7.5 0.7 %copy-done.7 = s32[48,1,128]{2,1,0:T(1,128)S(1)} copy-done((s32[48,1,128]{2,1,0:T(1,128)S(1)}, s32[48,1,128]{2,1,0:T(1,128)}, u32[]{:S(2)}) %copy-start.7) | copy-done | bytes 24600
  8.2 27.9 %shard_map.82 = f32[240,128]{1,0:T(8,128)S(1)} custom-call(f32[240,128]{1,0:T(8,128)S(1)} %bitcast.14, f32[240,128]{1,0:T(8,128)S(1)} %bitcast.15, f32[1200,128]{1,0:T(8,128)S(1)} %bitcast.10, f32[1200,128]{1,0:T(8,128)S(1)} %bitcast.11, f32[1200,128]{1,0:T(8,128)S(1)} %bitcast.12, f32[4800,128]{1,0:T(8,128)S(1)} %bitcast.9, s32[48,128]{1,0:T(8,128)S(1)} %bitcast.16, ...), custom_call_target="tpu_custom_call" | custom-call | flops 12000000 | bytes 5000000 | tf_op jit(solution)/shard_map/pallas_call | solution.py:391
  36.1 0.7 %copy.12 = f32[48,5,1,128]{3,2,1,0:T(1,128)} copy(f32[48,5,1,128]{3,2,1,0:T(1,128)S(1)} %bitcast.13) | data formatting | bytes 245760
Async XLA Ops:
  0.0 1.7 %copy-start = (f32[4,48,5,5,1,128]{5,4,3,2,1,0:T(1,128)S(1)}, f32[4,48,5,5,1,128]{5,4,3,2,1,0:T(1,128)}, u32[]{:S(2)}) copy-start(f32[4,48,5,5,1,128]{5,4,3,2,1,0:T(1,128)} %param.13) | copy-start | bytes 7372804
  1.7 1.1 %copy-start.1 = (f32[48,5,5,1,128]{4,3,2,1,0:T(1,128)S(1)}, f32[48,5,5,1,128]{4,3,2,1,0:T(1,128)}, u32[]{:S(2)}) copy-start(f32[48,5,5,1,128]{4,3,2,1,0:T(1,128)} %param.10) | copy-start | bytes 1843204
  2.8 1.1 %copy-start.2 = (f32[48,5,5,1,128]{4,3,2,1,0:T(1,128)S(1)}, f32[48,5,5,1,128]{4,3,2,1,0:T(1,128)}, u32[]{:S(2)}) copy-start(f32[48,5,5,1,128]{4,3,2,1,0:T(1,128)} %param.11) | copy-start | bytes 1843204
  3.8 1.1 %copy-start.3 = (f32[48,5,5,1,128]{4,3,2,1,0:T(1,128)S(1)}, f32[48,5,5,1,128]{4,3,2,1,0:T(1,128)}, u32[]{:S(2)}) copy-start(f32[48,5,5,1,128]{4,3,2,1,0:T(1,128)} %param.12) | copy-start | bytes 1843204
  4.9 0.9 %copy-start.4 = (f32[48,5,1,128]{3,2,1,0:T(1,128)S(1)}, f32[48,5,1,128]{3,2,1,0:T(1,128)}, u32[]{:S(2)}) copy-start(f32[48,5,1,128]{3,2,1,0:T(1,128)} %param.8) | copy-start | bytes 368644
  5.8 0.9 %copy-start.5 = (f32[48,5,1,128]{3,2,1,0:T(1,128)S(1)}, f32[48,5,1,128]{3,2,1,0:T(1,128)}, u32[]{:S(2)}) copy-start(f32[48,5,1,128]{3,2,1,0:T(1,128)} %param.9) | copy-start | bytes 368644
  6.7 0.7 %copy-start.6 = (s32[48,1,128]{2,1,0:T(1,128)S(1)}, s32[48,1,128]{2,1,0:T(1,128)}, u32[]{:S(2)}) copy-start(s32[48,1,128]{2,1,0:T(1,128)} %param.14) | copy-start | bytes 73732
  7.5 0.7 %copy-start.7 = (s32[48,1,128]{2,1,0:T(1,128)S(1)}, s32[48,1,128]{2,1,0:T(1,128)}, u32[]{:S(2)}) copy-start(s32[48,1,128]{2,1,0:T(1,128)} %param.15) | copy-start | bytes 73732
where the time goes:
time: 37.2 us; the launch traced here: 36.7 us
  Pallas kernels  27.9 us (75%)
  local copies, waits for them, and re-layouts  8.84 us (24%)
    pallas_call x1, Pallas kernels, per_device(): pl.pallas_call(functools.partial(kernel, sizes, J), out_shape=jax.ShapeDt...  27.9 us
    unnamed x17, local copies, waits for them, and re-layouts  8.84 us

commit v1 on v0

--- a/solution.py
+++ b/solution.py
@@ -30,6 +30,13 @@
 
 def vec_add(a, b):
     return [p + q for p, q in zip(a, b)]
+
+
+def lane_gather(row, index):
+    numbers = lax.GatherDimensionNumbers(
+        offset_dims=(), collapsed_slice_dims=(1,), start_index_map=(1,),
+        operand_batching_dims=(0,), start_indices_batching_dims=(0,))
+    return lax.gather(row, index[..., None], numbers, (1, 1), mode=lax.GatherScatterMode.PROMISE_IN_BOUNDS)
 
 
 def kernel(sizes, per_chunk, x_hbm, src_hbm, piv_hbm, low_hbm, upp_hbm, cpl_hbm, ibl_hbm, don_hbm, out_ref,
@@ -115,7 +122,7 @@
             rows = vec_rows(xb.at[sweep], j)
             for c in range(N):
                 i = j * N + c
-                packed = jnp.where(lane // 2 == i, pltpu.roll(rows[c], 2 * i + 1, 1), packed)
+                packed = jnp.where(lane >> 1 == i, pltpu.roll(rows[c], 2 * i + 1, 1), packed)
         edge_out[sweep] = packed
         copies = edge_copies(sweep)
         for copy in copies:
@@ -205,8 +212,8 @@
         if sweep == 0:
             ld_don.wait()
         places = [don[pl.ds(j, K, stride=J), :] for j in range(J)]
-        row_of = [p // LANES for p in places]
-        col_of = [p % LANES for p in places]
+        row_of = [p >> 7 for p in places]
+        col_of = [p & (LANES - 1) for p in places]
 
         def gather_step(r, carry):
             out = []
@@ -214,11 +221,11 @@
             for j in range(J):
                 hit = row_of[j] == r
                 for c in range(N):
-                    got = jnp.take_along_axis(rows[c], col_of[j], axis=1, mode="promise_in_bounds")
+                    got = lane_gather(rows[c], col_of[j])
                     out.append(jnp.where(hit, got, carry[j * N + c]))
             return out
 
-        got = lax.fori_loop(0, J * K, gather_step, [jnp.zeros((K, LANES), jnp.float32)] * (J * N))
+        got = lax.fori_loop(0, J * K, gather_step, [jnp.zeros((K, LANES), jnp.float32)] * (J * N), unroll=8)
         for i in range(J * N):
             donated[i] = got[i]
 
@@ -276,7 +283,7 @@
             return state
 
         zero = [jnp.zeros((K, LANES), jnp.float32)] * N
-        f = lax.fori_loop(0, J, forward_step, zero)
+        f = lax.fori_loop(0, J, forward_step, zero, unroll=True)
 
         def backward_step(i, state):
             j = J - 1 - i
@@ -286,7 +293,7 @@
                 work[j * N + c] = state[c]
             return state
 
-        b = lax.fori_loop(0, J, backward_step, zero)
+        b = lax.fori_loop(0, J, backward_step, zero, unroll=True)
         for level, s in enumerate(steps):
             f = vec_add(f, mat_vec(get_mat(scan_f, level), [pltpu.roll(v, s, 0) for v in f]))
         y_in = [jnp.where(chunk >= 1, pltpu.roll(v, 1, 0), 0.0) for v in f]
@@ -335,7 +342,7 @@
                 target[pl.ds(j * N + c, K, stride=J * N), :] = work[j * N + c] + more[c]
             return carry
 
-        lax.fori_loop(0, J, final_step, 0)
+        lax.fori_loop(0, J, final_step, 0, unroll=True)
         if sweep < SWEEPS - 1:
             span_now = span_copies(sweep + 1, xb.at[sweep + 1])
             for copy in span_now:
@@ -391,11 +398,11 @@
     out = pl.pallas_call(
         functools.partial(kernel, sizes, J),
         out_shape=jax.ShapeDtypeStruct((rows, LANES), f32),
-        in_specs=[pl.BlockSpec(memory_space=pl.ANY)] * 8,
+        in_specs=[pl.BlockSpec(memory_space=pltpu.HBM)] * 8,
         out_specs=pl.BlockSpec(memory_space=pltpu.VMEM),
         scratch_shapes=scratch,
         compiler_params=pltpu.CompilerParams(
-            collective_id=0, has_side_effects=True, vmem_limit_bytes=32 * 1024 * 1024),
+            collective_id=0, has_side_effects=True, vmem_limit_bytes=62 * 1024 * 1024),
         cost_estimate=pl.CostEstimate(flops=12000000, bytes_accessed=5000000, transcendentals=0),
     )(
         iterate.reshape(rows, lines), source.reshape(rows, lines), pivot.reshape(mats, lines),

time: 37.2 us -> 24.4 us (0.66)
  local copies, waits for them, and re-layouts: 8.84 us -> 1.58 us
  Pallas kernels: 27.9 us -> 22.7 us
    unnamed x17 -> x1, local copies, waits for them, and re-layouts: 8.84 us -> 1.58 us
    pallas_call x1, Pallas kernels: 27.9 us -> 22.7 us  [per_device(): pl.pallas_call(functools.partial(kernel, sizes, J), out_shape=jax.ShapeDt...]
where the time goes in v1:
time: 24.4 us; the launch traced here: 24.3 us
  Pallas kernels  22.7 us (93%)
  local copies, waits for them, and re-layouts  1.58 us (6%)
    pallas_call x1, Pallas kernels, per_device(): pl.pallas_call(functools.partial(kernel, sizes, J), out_shape=jax.ShapeDt...  22.7 us
    unnamed x1, local copies, waits for them, and re-layouts  1.58 us

profile of v1, /device:TPU:0, one launch (start us, length us, event | category | flops | bytes accessed | tf_op | source)
XLA Modules:
  0.0 24.3 jit_solution(15226013561424925183)
XLA Ops:
  0.0 22.7 %shard_map.82 = f32[240,128]{1,0:T(8,128)} custom-call(f32[240,128]{1,0:T(8,128)} %bitcast.14, f32[240,128]{1,0:T(8,128)} %bitcast.15, f32[1200,128]{1,0:T(8,128)} %bitcast.10, f32[1200,128]{1,0:T(8,128)} %bitcast.11, f32[1200,128]{1,0:T(8,128)} %bitcast.12, f32[4800,128]{1,0:T(8,128)} %bitcast.9, s32[48,128]{1,0:T(8,128)} %bitcast.16, s32[48,128]{1,0:T(8,128)} %bitcast.17), custom_call_target="tpu_custom_call" | custom-call | flops 12000000 | bytes 5000000 | tf_op jit(solution)/shard_map/pallas_call | solution.py:398
  22.7 1.6 %copy.12 = f32[48,5,1,128]{3,2,1,0:T(1,128)} copy(f32[48,5,1,128]{3,2,1,0:T(1,128)} %bitcast.13) | data formatting | bytes 245760

commit v2 on v1

--- a/solution.py
+++ b/solution.py
@@ -40,9 +40,9 @@
 
 
 def kernel(sizes, per_chunk, x_hbm, src_hbm, piv_hbm, low_hbm, upp_hbm, cpl_hbm, ibl_hbm, don_hbm, out_ref,
-           xb, src, piv, low, upp, cpl, ibl, don, plane, edge_out, edge_in, vec_all, map_all,
+           xb, xk, src, piv, low, upp, cpl, ibl, don, plane, plane_k, edge_out, edge_in, vec_all, map_all,
            fw, gw, bw, scan_f, scan_b, excl, base, work, donated,
-           load_sem, span_send, span_recv, edge_send, edge_recv, vec_send, vec_recv, map_send, map_recv):
+           load_sem, span_send, span_recv, piece_send, piece_recv, edge_send, edge_recv, vec_send, vec_recv, map_send, map_recv):
     J = per_chunk
     n_normal, n_span, n_stream = sizes
     me, sp, st = lax.axis_index("normal"), lax.axis_index("span"), lax.axis_index("stream")
@@ -50,7 +50,7 @@
     stream_targets = [lax.rem(st + 1, n_stream)] if n_stream == 2 else [lax.rem(st + 1, n_stream), lax.rem(st + n_stream - 1, n_stream)]
     sides_span, sides_stream = len(span_targets), len(stream_targets)
 
-    pairs = [(x_hbm, xb.at[0]), (low_hbm, low), (upp_hbm, upp), (don_hbm, don), (cpl_hbm, cpl),
+    pairs = [(x_hbm, xb), (low_hbm, low), (upp_hbm, upp), (don_hbm, don), (cpl_hbm, cpl),
              (src_hbm, src), (ibl_hbm, ibl), (piv_hbm, piv)]
     loads = [pltpu.make_async_copy(a, b, load_sem.at[i]) for i, (a, b) in enumerate(pairs)]
     for load in loads:
@@ -66,11 +66,23 @@
         pl.semaphore_signal(barrier, inc=1, device_id={"normal": lax.rem(me + o, n_normal)}, device_id_type=MESH)
     pl.semaphore_wait(barrier, sides_span + sides_stream + n_normal - 1)
 
-    def span_copies(sweep, source):
+    def span_copies():
         return [
             pltpu.make_async_remote_copy(
-                src_ref=source, dst_ref=plane.at[sweep, i], send_sem=span_send.at[sweep, i],
-                recv_sem=span_recv.at[sweep, i], device_id={"span": t}, device_id_type=MESH)
+                src_ref=x_hbm, dst_ref=plane.at[i], send_sem=span_send.at[i],
+                recv_sem=span_recv.at[i], device_id={"span": t}, device_id_type=MESH)
+            for i, t in enumerate(span_targets)
+        ]
+
+    group = 2 if J % 2 == 0 else 1
+
+    def piece_copies(sweep, piece):
+        part = pl.ds(piece * group * N, group * N)
+        return [
+            pltpu.make_async_remote_copy(
+                src_ref=xk.at[sweep - 1, part], dst_ref=plane_k.at[sweep - 1, i, part],
+                send_sem=piece_send.at[sweep - 1, piece, i], recv_sem=piece_recv.at[sweep - 1, piece, i],
+                device_id={"span": t}, device_id_type=MESH)
             for i, t in enumerate(span_targets)
         ]
 
@@ -116,10 +128,15 @@
             for e in range(N):
                 ref[(*at, c, e)] = mat[c][e]
 
+    def x_rows(sweep, j):
+        if sweep == 0:
+            return vec_rows(xb, j)
+        return [xk[sweep - 1, j * N + c] for c in range(N)]
+
     def send_edges(sweep):
         packed = jnp.zeros((K, LANES), jnp.float32)
         for j in range(J):
-            rows = vec_rows(xb.at[sweep], j)
+            rows = x_rows(sweep, j)
             for c in range(N):
                 i = j * N + c
                 packed = jnp.where(lane >> 1 == i, pltpu.roll(rows[c], 2 * i + 1, 1), packed)
@@ -129,7 +146,7 @@
             copy.start()
         return copies
 
-    span_now = span_copies(0, x_hbm)
+    span_now = span_copies()
     for copy in span_now:
         copy.start()
     ld_x.wait()
@@ -208,24 +225,28 @@
     pending += map_now
 
     for sweep in range(SWEEPS):
-        here = xb.at[sweep]
         if sweep == 0:
             ld_don.wait()
         places = [don[pl.ds(j, K, stride=J), :] for j in range(J)]
         row_of = [p >> 7 for p in places]
         col_of = [p & (LANES - 1) for p in places]
 
-        def gather_step(r, carry):
-            out = []
-            rows = [jnp.broadcast_to(here[pl.ds(r * N + c, 1), :], (K, LANES)) for c in range(N)]
-            for j in range(J):
-                hit = row_of[j] == r
-                for c in range(N):
-                    got = lane_gather(rows[c], col_of[j])
-                    out.append(jnp.where(hit, got, carry[j * N + c]))
-            return out
-
-        got = lax.fori_loop(0, J * K, gather_step, [jnp.zeros((K, LANES), jnp.float32)] * (J * N), unroll=8)
+        def gather_step(jj, carry):
+            carry = list(carry)
+            for k in range(K):
+                if sweep == 0:
+                    ones = [xb[pl.ds((k * J + jj) * N + c, 1), :] for c in range(N)]
+                else:
+                    ones = [xk[sweep - 1, jj * N + c, k:k + 1, :] for c in range(N)]
+                rows = [jnp.broadcast_to(one, (K, LANES)) for one in ones]
+                for j in range(J):
+                    hit = row_of[j] == k * J + jj
+                    for c in range(N):
+                        got = lane_gather(rows[c], col_of[j])
+                        carry[j * N + c] = jnp.where(hit, got, carry[j * N + c])
+            return carry
+
+        got = lax.fori_loop(0, J, gather_step, [jnp.zeros((K, LANES), jnp.float32)] * (J * N))
         for i in range(J * N):
             donated[i] = got[i]
 
@@ -238,7 +259,7 @@
         right = edge_in[sweep, sides_stream - 1]
         lows, highs = [], []
         for j in range(J):
-            rows = vec_rows(here, j)
+            rows = x_rows(sweep, j)
             flag = ibl[pl.ds(j, K, stride=J), :]
             lows, highs = [], []
             for c in range(N):
@@ -254,16 +275,20 @@
                     acc = acc - (c2[e][c] * lows[e] + c3[e][c] * highs[e])
                 base[j * N + c] = acc
 
-        for copy in span_now:
-            copy.wait_recv()
         if sweep == 0:
+            for copy in span_now:
+                copy.wait_recv()
             ld_piv.wait()
 
         def forward_step(j, state):
             c0 = mat_rows(cpl, j)
             c1 = mat_rows(cpl, j, J * K * N * N)
             flag = ibl[pl.ds(j, K, stride=J), :]
-            x0 = vec_rows(plane.at[sweep, 0], j)
+            if sweep == 0:
+                sides = [vec_rows(plane.at[i], j) for i in range(sides_span)]
+            else:
+                sides = [[plane_k[sweep - 1, i, j * N + c] for c in range(N)] for i in range(sides_span)]
+            x0 = sides[0]
             rhs = []
             if sides_span == 1:
                 both = mat_map(jnp.add, c0, c1)
@@ -271,7 +296,7 @@
                     acc = functools.reduce(jnp.add, [both[e][c] * x0[e] for e in range(N)])
                     rhs.append(jnp.where(flag == 0, 0.0, base[j * N + c] - acc))
             else:
-                x1 = vec_rows(plane.at[sweep, 1], j)
+                x1 = sides[1]
                 for c in range(N):
                     acc = functools.reduce(jnp.add, [c0[e][c] * x0[e] + c1[e][c] * x1[e] for e in range(N)])
                     rhs.append(jnp.where(flag == 0, 0.0, base[j * N + c] - acc))
@@ -283,7 +308,12 @@
             return state
 
         zero = [jnp.zeros((K, LANES), jnp.float32)] * N
-        f = lax.fori_loop(0, J, forward_step, zero, unroll=True)
+        f = zero
+        for j in range(J):
+            if sweep > 0 and j % group == 0:
+                for copy in piece_copies(sweep, j // group):
+                    copy.wait_recv()
+            f = forward_step(j, f)
 
         def backward_step(i, state):
             j = J - 1 - i
@@ -334,21 +364,22 @@
         x_in = vec_add(x_in, mat_vec(get_mat(excl, 1), y_entry))
         x_in = vec_add(x_in, mat_vec(get_mat(excl, 2), x_entry))
 
-        target = out_ref if sweep == SWEEPS - 1 else xb.at[sweep + 1]
-
-        def final_step(j, carry):
+        for j in range(J):
             more = vec_add(mat_vec(get_mat(gw, j), y_in), mat_vec(get_mat(bw, j), x_in))
             for c in range(N):
-                target[pl.ds(j * N + c, K, stride=J * N), :] = work[j * N + c] + more[c]
-            return carry
-
-        lax.fori_loop(0, J, final_step, 0, unroll=True)
+                value = work[j * N + c] + more[c]
+                if sweep == SWEEPS - 1:
+                    out_ref[pl.ds(j * N + c, K, stride=J * N), :] = value
+                else:
+                    xk[sweep, j * N + c] = value
+            if sweep < SWEEPS - 1 and j % group == group - 1:
+                copies = piece_copies(sweep + 1, j // group)
+                for copy in copies:
+                    copy.start()
+                pending += copies
         if sweep < SWEEPS - 1:
-            span_now = span_copies(sweep + 1, xb.at[sweep + 1])
-            for copy in span_now:
-                copy.start()
             edge_now = send_edges(sweep + 1)
-            pending += list(span_now) + list(edge_now)
+            pending += edge_now
 
     for copy in pending:
         copy.wait_send()
@@ -363,7 +394,8 @@
     f32 = jnp.float32
     peers = max(n_normal - 1, 1)
     scratch = [
-        pltpu.VMEM((SWEEPS, rows, LANES), f32),
+        pltpu.VMEM((rows, LANES), f32),
+        pltpu.VMEM((SWEEPS - 1, J * N, K, LANES), f32),
         pltpu.VMEM((rows, LANES), f32),
         pltpu.VMEM((mats, LANES), f32),
         pltpu.VMEM((mats, LANES), f32),
@@ -371,7 +403,8 @@
         pltpu.VMEM((4 * mats, LANES), f32),
         pltpu.VMEM((points, LANES), jnp.int32),
         pltpu.VMEM((points, LANES), jnp.int32),
-        pltpu.VMEM((SWEEPS, sides_span, rows, LANES), f32),
+        pltpu.VMEM((sides_span, rows, LANES), f32),
+        pltpu.VMEM((SWEEPS - 1, sides_span, J * N, K, LANES), f32),
         pltpu.VMEM((SWEEPS, K, LANES), f32),
         pltpu.VMEM((SWEEPS, sides_stream, K, LANES), f32),
         pltpu.VMEM((SWEEPS, n_normal, 2 * K, LANES), f32),
@@ -386,8 +419,10 @@
         pltpu.VMEM((J * N, K, LANES), f32),
         pltpu.VMEM((J * N, K, LANES), f32),
         pltpu.SemaphoreType.DMA((8,)),
-        pltpu.SemaphoreType.DMA((SWEEPS, sides_span)),
-        pltpu.SemaphoreType.DMA((SWEEPS, sides_span)),
+        pltpu.SemaphoreType.DMA((sides_span,)),
+        pltpu.SemaphoreType.DMA((sides_span,)),
+        pltpu.SemaphoreType.DMA((SWEEPS - 1, J, sides_span)),
+        pltpu.SemaphoreType.DMA((SWEEPS - 1, J, sides_span)),
         pltpu.SemaphoreType.DMA((SWEEPS, sides_stream)),
         pltpu.SemaphoreType.DMA((SWEEPS, sides_stream)),
         pltpu.SemaphoreType.DMA((SWEEPS, peers)),
@@ -397,18 +432,19 @@
     ]
     out = pl.pallas_call(
         functools.partial(kernel, sizes, J),
-        out_shape=jax.ShapeDtypeStruct((rows, LANES), f32),
+        out_shape=pltpu.VMEM((rows, LANES), f32),
         in_specs=[pl.BlockSpec(memory_space=pltpu.HBM)] * 8,
         out_specs=pl.BlockSpec(memory_space=pltpu.VMEM),
         scratch_shapes=scratch,
         compiler_params=pltpu.CompilerParams(
-            collective_id=0, has_side_effects=True, vmem_limit_bytes=62 * 1024 * 1024),
+            collective_id=0, has_side_effects=True, vmem_limit_bytes=32 * 1024 * 1024),
         cost_estimate=pl.CostEstimate(flops=12000000, bytes_accessed=5000000, transcendentals=0),
-    )(
-        iterate.reshape(rows, lines), source.reshape(rows, lines), pivot.reshape(mats, lines),
-        lower.reshape(mats, lines), upper.reshape(mats, lines), coupling.reshape(4 * mats, lines),
-        iblank.reshape(points, lines), donor.reshape(points, lines),
-    )
+    )(*[
+        pltpu.with_memory_space_constraint(operand, pltpu.HBM) for operand in (
+            iterate.reshape(rows, lines), source.reshape(rows, lines), pivot.reshape(mats, lines),
+            lower.reshape(mats, lines), upper.reshape(mats, lines), coupling.reshape(4 * mats, lines),
+            iblank.reshape(points, lines), donor.reshape(points, lines))
+    ])
     return out.reshape(points, comps, planes, lines)
 
 

time: 24.4 us -> 22.8 us (0.934)
  local copies, waits for them, and re-layouts: 1.58 us -> 0.65 us
  Pallas kernels: 22.7 us -> 22 us
    unnamed x1, local copies, waits for them, and re-layouts: 1.58 us -> 0.65 us
    pallas_call x1, Pallas kernels: 22.7 us -> 22 us  [per_device(): pl.pallas_call(functools.partial(kernel, sizes, J), out_shape=pltpu.VMEM(...]
where the time goes in v2:
time: 22.8 us; the launch traced here: 22.6 us
  Pallas kernels  22 us (96%)
  local copies, waits for them, and re-layouts  0.65 us (3%)
    pallas_call x1, Pallas kernels, per_device(): pl.pallas_call(functools.partial(kernel, sizes, J), out_shape=pltpu.VMEM(...  22 us
    unnamed x1, local copies, waits for them, and re-layouts  0.65 us

profile of v2, /device:TPU:0, one launch (start us, length us, event | category | flops | bytes accessed | tf_op | source)
XLA Modules:
  0.0 22.6 jit_solution(14146419800576311823)
XLA Ops:
  0.0 22.0 %shard_map.82 = f32[240,128]{1,0:T(8,128)S(1)} custom-call(f32[240,128]{1,0:T(8,128)} %bitcast.14, f32[240,128]{1,0:T(8,128)} %bitcast.15, f32[1200,128]{1,0:T(8,128)} %bitcast.11, f32[1200,128]{1,0:T(8,128)} %bitcast.12, f32[1200,128]{1,0:T(8,128)} %bitcast.13, f32[4800,128]{1,0:T(8,128)} %bitcast.10, s32[48,128]{1,0:T(8,128)} %bitcast.16, s32[48,128]{1,0:T(8,128)} %bitcast.17), custom_call_target="tpu_custom_call" | custom-call | flops 12000000 | bytes 5000000 | tf_op jit(solution)/shard_map/pallas_call | solution.py:433
  22.0 0.7 %copy.12 = f32[48,5,1,128]{3,2,1,0:T(1,128)} copy(f32[48,5,1,128]{3,2,1,0:T(1,128)S(1)} %bitcast.9) | data formatting | bytes 245760

commit v3 on v2

--- a/solution.py
+++ b/solution.py
@@ -13,13 +13,19 @@
 MESH = pl.DeviceIdType.MESH
 
 
+def tree_sum(terms):
+    while len(terms) > 1:
+        terms = [a + b for a, b in zip(terms[::2], terms[1::2])] + ([terms[-1]] if len(terms) % 2 else [])
+    return terms[0]
+
+
 def mat_vec(mat, vec):
-    return [functools.reduce(jnp.add, [mat[c][e] * vec[e] for e in range(N)]) for c in range(N)]
+    return [tree_sum([mat[c][e] * vec[e] for e in range(N)]) for c in range(N)]
 
 
 def mat_mat(left, right):
     return [
-        [functools.reduce(jnp.add, [left[c][e] * right[e][f] for e in range(N)]) for f in range(N)]
+        [tree_sum([left[c][e] * right[e][f] for e in range(N)]) for f in range(N)]
         for c in range(N)
     ]
 
@@ -153,6 +159,32 @@
     edge_now = send_edges(0)
     pending = list(span_now) + list(edge_now)
 
+    def gather_donors(sweep):
+        places = [don[pl.ds(j, K, stride=J), :] for j in range(J)]
+        row_of = [p >> 7 for p in places]
+        col_of = [p & (LANES - 1) for p in places]
+
+        def gather_step(jj, carry):
+            carry = list(carry)
+            for k in range(K):
+                if sweep == 0:
+                    ones = [xb[pl.ds((k * J + jj) * N + c, 1), :] for c in range(N)]
+                else:
+                    ones = [xk[sweep - 1, jj * N + c, k:k + 1, :] for c in range(N)]
+                rows = [jnp.broadcast_to(one, (K, LANES)) for one in ones]
+                for j in range(J):
+                    hit = row_of[j] == k * J + jj
+                    for c in range(N):
+                        got = lane_gather(rows[c], col_of[j])
+                        carry[j * N + c] = jnp.where(hit, got, carry[j * N + c])
+            return carry
+
+        got = lax.fori_loop(0, J, gather_step, [jnp.zeros((K, LANES), jnp.float32)] * (J * N))
+        for i in range(J * N):
+            donated[i] = got[i]
+
+    ld_don.wait()
+    gather_donors(0)
     ld_low.wait()
     ld_upp.wait()
 
@@ -169,21 +201,16 @@
     put_mat(bw, start_b, J - 1)
     put_mat(gw, last_f, J - 1)
 
-    def bw_step(i, carry):
+    def back_step(i, carry):
         j = J - 2 - i
-        carry = mat_mat(mat_map(lambda a: -a, mat_rows(upp, j)), carry)
-        put_mat(bw, carry, j)
-        return carry
-
-    def gw_step(i, carry):
-        j = J - 2 - i
-        moved = mat_mat(mat_rows(upp, j), carry)
-        carry = mat_map(lambda a, b: a - b, get_mat(fw, j), moved)
-        put_mat(gw, carry, j)
-        return carry
-
-    first_b = lax.fori_loop(0, J - 1, bw_step, start_b)
-    first_g = lax.fori_loop(0, J - 1, gw_step, last_f)
+        block = mat_rows(upp, j)
+        b_now = mat_map(lambda a: -a, mat_mat(block, carry[0]))
+        g_now = mat_map(lambda a, b: a - b, get_mat(fw, j), mat_mat(block, carry[1]))
+        put_mat(bw, b_now, j)
+        put_mat(gw, g_now, j)
+        return b_now, g_now
+
+    first_b, first_g = lax.fori_loop(0, J - 1, back_step, (start_b, last_f))
 
     steps = (1, 2, 4)
     whole = last_f
@@ -225,31 +252,8 @@
     pending += map_now
 
     for sweep in range(SWEEPS):
-        if sweep == 0:
-            ld_don.wait()
-        places = [don[pl.ds(j, K, stride=J), :] for j in range(J)]
-        row_of = [p >> 7 for p in places]
-        col_of = [p & (LANES - 1) for p in places]
-
-        def gather_step(jj, carry):
-            carry = list(carry)
-            for k in range(K):
-                if sweep == 0:
-                    ones = [xb[pl.ds((k * J + jj) * N + c, 1), :] for c in range(N)]
-                else:
-                    ones = [xk[sweep - 1, jj * N + c, k:k + 1, :] for c in range(N)]
-                rows = [jnp.broadcast_to(one, (K, LANES)) for one in ones]
-                for j in range(J):
-                    hit = row_of[j] == k * J + jj
-                    for c in range(N):
-                        got = lane_gather(rows[c], col_of[j])
-                        carry[j * N + c] = jnp.where(hit, got, carry[j * N + c])
-            return carry
-
-        got = lax.fori_loop(0, J, gather_step, [jnp.zeros((K, LANES), jnp.float32)] * (J * N))
-        for i in range(J * N):
-            donated[i] = got[i]
-
+        if sweep > 0:
+            gather_donors(sweep)
         if sweep == 0:
             for load in (ld_src, ld_ibl, ld_cpl):
                 load.wait()
@@ -293,12 +297,12 @@
             if sides_span == 1:
                 both = mat_map(jnp.add, c0, c1)
                 for c in range(N):
-                    acc = functools.reduce(jnp.add, [both[e][c] * x0[e] for e in range(N)])
+                    acc = tree_sum([both[e][c] * x0[e] for e in range(N)])
                     rhs.append(jnp.where(flag == 0, 0.0, base[j * N + c] - acc))
             else:
                 x1 = sides[1]
                 for c in range(N):
-                    acc = functools.reduce(jnp.add, [c0[e][c] * x0[e] + c1[e][c] * x1[e] for e in range(N)])
+                    acc = tree_sum([c0[e][c] * x0[e] + c1[e][c] * x1[e] for e in range(N)])
                     rhs.append(jnp.where(flag == 0, 0.0, base[j * N + c] - acc))
             scaled = mat_vec(mat_rows(piv, j), rhs)
             moved = mat_vec(mat_rows(low, j), state)
@@ -345,7 +349,7 @@
             copy.wait_recv()
 
         def apply_map(d, m, state):
-            return functools.reduce(jnp.add, [
+            return tree_sum([
                 map_all[d, pl.ds(m * N * N + e, N, stride=N), :] * state[e:e + 1] for e in range(N)])
 
         none = jnp.zeros((N, LANES), jnp.float32)

time: 22.8 us -> 24.3 us (1.066)
  Pallas kernels: 22 us -> 23.5 us
    pallas_call x1, Pallas kernels: 22 us -> 23.5 us  [per_device(): pl.pallas_call(functools.partial(kernel, sizes, J), out_shape=pltpu.VMEM(...]
where the time goes in v3:
time: 24.3 us; the launch traced here: 24.1 us
  Pallas kernels  23.5 us (97%)
  local copies, waits for them, and re-layouts  0.65 us (3%)
    pallas_call x1, Pallas kernels, per_device(): pl.pallas_call(functools.partial(kernel, sizes, J), out_shape=pltpu.VMEM(...  23.5 us
    unnamed x1, local copies, waits for them, and re-layouts  0.65 us

profile of v3, /device:TPU:0, one launch (start us, length us, event | category | flops | bytes accessed | tf_op | source)
XLA Modules:
  0.0 24.1 jit_solution(9078854643583813250)
XLA Ops:
  0.0 23.5 %shard_map.82 = f32[240,128]{1,0:T(8,128)S(1)} custom-call(f32[240,128]{1,0:T(8,128)} %bitcast.14, f32[240,128]{1,0:T(8,128)} %bitcast.15, f32[1200,128]{1,0:T(8,128)} %bitcast.11, f32[1200,128]{1,0:T(8,128)} %bitcast.12, f32[1200,128]{1,0:T(8,128)} %bitcast.13, f32[4800,128]{1,0:T(8,128)} %bitcast.10, s32[48,128]{1,0:T(8,128)} %bitcast.16, s32[48,128]{1,0:T(8,128)} %bitcast.17), custom_call_target="tpu_custom_call" | custom-call | flops 12000000 | bytes 5000000 | tf_op jit(solution)/shard_map/pallas_call | solution.py:437
  23.5 0.7 %copy.12 = f32[48,5,1,128]{3,2,1,0:T(1,128)} copy(f32[48,5,1,128]{3,2,1,0:T(1,128)S(1)} %bitcast.9) | data formatting | bytes 245760

commit v4 on v2

--- a/solution.py
+++ b/solution.py
@@ -13,8 +13,14 @@
 MESH = pl.DeviceIdType.MESH
 
 
+def tree_sum(terms):
+    while len(terms) > 1:
+        terms = [a + b for a, b in zip(terms[::2], terms[1::2])] + ([terms[-1]] if len(terms) % 2 else [])
+    return terms[0]
+
+
 def mat_vec(mat, vec):
-    return [functools.reduce(jnp.add, [mat[c][e] * vec[e] for e in range(N)]) for c in range(N)]
+    return [tree_sum([mat[c][e] * vec[e] for e in range(N)]) for c in range(N)]
 
 
 def mat_mat(left, right):
@@ -110,6 +116,30 @@
                 src_ref=ref.at[me], dst_ref=ref.at[came], send_sem=sends.at[o - 1], recv_sem=recvs.at[o - 1],
                 device_id={"normal": lax.rem(me + o, n_normal)}, device_id_type=MESH))
         return out
+
+    def map_copies(part, arriving):
+        out = []
+        for o in range(1, n_normal):
+            slot = lax.rem(me + n_normal - o, n_normal) if arriving else me
+            copy = pltpu.make_async_remote_copy(
+                src_ref=map_all.at[part, me], dst_ref=map_all.at[part, slot],
+                send_sem=map_send.at[part, o - 1], recv_sem=map_recv.at[part, o - 1],
+                device_id={"normal": lax.rem(me + o, n_normal)}, device_id_type=MESH)
+            if part == 0:
+                used = slot < n_normal - 1
+            else:
+                used = me - o < 0 if arriving else me + o >= n_normal
+            out.append((used, copy))
+        return out
+
+    def send_map(part, mat, row):
+        for c in range(N):
+            for e in range(N):
+                map_all[part, me, pl.ds(c * N + e, 1), :] = mat[c][e][row:row + 1]
+        for used, copy in map_copies(part, False):
+            @pl.when(used)
+            def _(copy=copy):
+                copy.start()
 
     lane = lax.broadcasted_iota(jnp.int32, (K, LANES), 1)
     chunk = lax.broadcasted_iota(jnp.int32, (K, LANES), 0)
@@ -153,8 +183,13 @@
     edge_now = send_edges(0)
     pending = list(span_now) + list(edge_now)
 
+    for part in (1, 2):
+        for d in range(n_normal - 1):
+            @pl.when(d < me)
+            def _(part=part, d=d):
+                map_all[part, d] = jnp.zeros((N * N, LANES), jnp.float32)
+
     ld_low.wait()
-    ld_upp.wait()
 
     first = mat_map(lambda a: -a, mat_rows(low, 0))
     put_mat(fw, first, 0)
@@ -165,6 +200,17 @@
         return carry
 
     last_f = lax.fori_loop(1, J, fw_step, first)
+    steps = (1, 2, 4)
+    whole = last_f
+    for level, s in enumerate(steps):
+        put_mat(scan_f, mat_map(lambda a: jnp.where(chunk >= s, a, 0.0), whole), level)
+        moved = mat_mat(whole, mat_map(lambda a: pltpu.roll(a, s, 0), whole))
+        whole = mat_map(lambda a, b: jnp.where(chunk >= s, b, a), whole, moved)
+    send_map(0, whole, K - 1)
+    before = mat_map(lambda a: pltpu.roll(a, 1, 0), whole)
+    before = [[jnp.where(chunk >= 1, before[c][e], 1.0 if c == e else 0.0) for e in range(N)] for c in range(N)]
+    put_mat(excl, before, 0)
+    ld_upp.wait()
     start_b = mat_map(lambda a: -a, mat_rows(upp, J - 1))
     put_mat(bw, start_b, J - 1)
     put_mat(gw, last_f, J - 1)
@@ -185,18 +231,6 @@
     first_b = lax.fori_loop(0, J - 1, bw_step, start_b)
     first_g = lax.fori_loop(0, J - 1, gw_step, last_f)
 
-    steps = (1, 2, 4)
-    whole = last_f
-    for level, s in enumerate(steps):
-        put_mat(scan_f, mat_map(lambda a: jnp.where(chunk >= s, a, 0.0), whole), level)
-        moved = mat_mat(whole, mat_map(lambda a: pltpu.roll(a, s, 0), whole))
-        whole = mat_map(lambda a, b: jnp.where(chunk >= s, b, a), whole, moved)
-    before = mat_map(lambda a: pltpu.roll(a, 1, 0), whole)
-    before = [[jnp.where(chunk >= 1, before[c][e], 1.0 if c == e else 0.0) for e in range(N)] for c in range(N)]
-    put_mat(excl, before, 0)
-    for c in range(N):
-        for e in range(N):
-            map_all[me, pl.ds(c * N + e, 1), :] = whole[c][e][K - 1:K]
     seen = mat_mat(first_g, before)
     put_mat(excl, seen, 1)
 
@@ -205,24 +239,16 @@
         put_mat(scan_b, mat_map(lambda a: jnp.where(chunk < K - s, a, 0.0), whole), level)
         moved = mat_mat(whole, mat_map(lambda a: pltpu.roll(a, K - s, 0), whole))
         whole = mat_map(lambda a, b: jnp.where(chunk < K - s, b, a), whole, moved)
+    send_map(1, whole, 0)
     after = mat_map(lambda a: pltpu.roll(a, K - 1, 0), whole)
     after = [[jnp.where(chunk < K - 1, after[c][e], 1.0 if c == e else 0.0) for e in range(N)] for c in range(N)]
     put_mat(excl, after, 2)
-    for c in range(N):
-        for e in range(N):
-            map_all[me, pl.ds(N * N + c * N + e, 1), :] = whole[c][e][0:1]
     seen = get_mat(excl, 1)
     for level, s in enumerate(steps):
         moved = mat_mat(get_mat(scan_b, level), mat_map(lambda a: pltpu.roll(a, K - s, 0), seen))
         seen = mat_map(jnp.add, seen, moved)
-    for c in range(N):
-        for e in range(N):
-            map_all[me, pl.ds(2 * N * N + c * N + e, 1), :] = seen[c][e][0:1]
+    send_map(2, seen, 0)
     put_mat(excl, mat_map(lambda a: jnp.where(chunk < K - 1, pltpu.roll(a, K - 1, 0), 0.0), seen), 1)
-    map_now = normal_copies(map_all, map_send, map_recv)
-    for copy in map_now:
-        copy.start()
-    pending += map_now
 
     for sweep in range(SWEEPS):
         if sweep == 0:
@@ -339,14 +365,17 @@
             copy.start()
         pending += sends
         if sweep == 0:
-            for copy in normal_arrivals(map_all, map_send, map_recv):
-                copy.wait_recv()
+            for part in range(3):
+                for used, copy in map_copies(part, True):
+                    @pl.when(used)
+                    def _(copy=copy):
+                        copy.wait_recv()
         for copy in normal_arrivals(vec_all.at[sweep], vec_send.at[sweep], vec_recv.at[sweep]):
             copy.wait_recv()
 
         def apply_map(d, m, state):
             return functools.reduce(jnp.add, [
-                map_all[d, pl.ds(m * N * N + e, N, stride=N), :] * state[e:e + 1] for e in range(N)])
+                map_all[m, d, pl.ds(e, N, stride=N), :] * state[e:e + 1] for e in range(N)])
 
         none = jnp.zeros((N, LANES), jnp.float32)
         entries, state, mine = [none], none, none
@@ -383,6 +412,11 @@
 
     for copy in pending:
         copy.wait_send()
+    for part in range(3):
+        for used, copy in map_copies(part, False):
+            @pl.when(used)
+            def _(copy=copy):
+                copy.wait_send()
 
 
 def per_device(sizes, iterate, source, pivot, lower, upper, coupling, iblank, donor):
@@ -408,7 +442,7 @@
         pltpu.VMEM((SWEEPS, K, LANES), f32),
         pltpu.VMEM((SWEEPS, sides_stream, K, LANES), f32),
         pltpu.VMEM((SWEEPS, n_normal, 2 * K, LANES), f32),
-        pltpu.VMEM((n_normal, 80, LANES), f32),
+        pltpu.VMEM((3, n_normal, N * N, LANES), f32),
         pltpu.VMEM((J, N, N, K, LANES), f32),
         pltpu.VMEM((J, N, N, K, LANES), f32),
         pltpu.VMEM((J, N, N, K, LANES), f32),
@@ -427,8 +461,8 @@
         pltpu.SemaphoreType.DMA((SWEEPS, sides_stream)),
         pltpu.SemaphoreType.DMA((SWEEPS, peers)),
         pltpu.SemaphoreType.DMA((SWEEPS, peers)),
-        pltpu.SemaphoreType.DMA((peers,)),
-        pltpu.SemaphoreType.DMA((peers,)),
+        pltpu.SemaphoreType.DMA((3, peers)),
+        pltpu.SemaphoreType.DMA((3, peers)),
     ]
     out = pl.pallas_call(
         functools.partial(kernel, sizes, J),

time: 22.8 us -> 22.9 us (level)
  no operation moved by 1% of the time
where the time goes in v4:
time: 22.9 us; the launch traced here: 22.8 us
  Pallas kernels  22.1 us (97%)
  local copies, waits for them, and re-layouts  0.65 us (3%)
    pallas_call x1, Pallas kernels, per_device(): pl.pallas_call(functools.partial(kernel, sizes, J), out_shape=pltpu.VMEM(...  22.1 us
    unnamed x1, local copies, waits for them, and re-layouts  0.65 us

profile of v4, /device:TPU:0, one launch (start us, length us, event | category | flops | bytes accessed | tf_op | source)
XLA Modules:
  0.0 22.8 jit_solution(3723739705603738619)
XLA Ops:
  0.0 22.1 %shard_map.82 = f32[240,128]{1,0:T(8,128)S(1)} custom-call(f32[240,128]{1,0:T(8,128)} %bitcast.14, f32[240,128]{1,0:T(8,128)} %bitcast.15, f32[1200,128]{1,0:T(8,128)} %bitcast.11, f32[1200,128]{1,0:T(8,128)} %bitcast.12, f32[1200,128]{1,0:T(8,128)} %bitcast.13, f32[4800,128]{1,0:T(8,128)} %bitcast.10, s32[48,128]{1,0:T(8,128)} %bitcast.16, s32[48,128]{1,0:T(8,128)} %bitcast.17), custom_call_target="tpu_custom_call" | custom-call | flops 12000000 | bytes 5000000 | tf_op jit(solution)/shard_map/pallas_call | solution.py:467
  22.1 0.7 %copy.12 = f32[48,5,1,128]{3,2,1,0:T(1,128)} copy(f32[48,5,1,128]{3,2,1,0:T(1,128)S(1)} %bitcast.9) | data formatting | bytes 245760

commit v5 on v4

--- a/solution.py
+++ b/solution.py
@@ -23,11 +23,18 @@
     return [tree_sum([mat[c][e] * vec[e] for e in range(N)]) for c in range(N)]
 
 
-def mat_mat(left, right):
-    return [
-        [functools.reduce(jnp.add, [left[c][e] * right[e][f] for e in range(N)]) for f in range(N)]
-        for c in range(N)
-    ]
+def mat_mat(left_row, right, finish):
+    out = []
+    for c in range(N):
+        row = left_row(c)
+        sums = []
+        for f in range(N):
+            total = row[0] * right[0][f]
+            for e in range(1, N):
+                total = total + row[e] * right[e][f]
+            sums.append(total)
+        out.append(finish(c, sums))
+    return out
 
 
 def mat_map(function, *mats):
@@ -150,6 +157,26 @@
     def mat_rows(ref, j, first=0):
         return [[ref[pl.ds(first + j * N * N + c * N + e, K, stride=J * N * N), :] for e in range(N)] for c in range(N)]
 
+    def block_row(ref, j):
+        return lambda c: [ref[pl.ds(j * N * N + c * N + e, K, stride=J * N * N), :] for e in range(N)]
+
+    def kept_row(ref, *at):
+        return lambda c: [ref[(*at, c, e)] for e in range(N)]
+
+    def keep(ref, *at, sign=1):
+        def finish(c, sums):
+            sums = [-v for v in sums] if sign < 0 else sums
+            for e in range(N):
+                ref[(*at, c, e)] = sums[e]
+            return sums
+        return finish
+
+    def double(scan, level, whole, shift, mask):
+        put_mat(scan, mat_map(lambda a: jnp.where(mask, a, 0.0), whole), level)
+        rolled = mat_map(lambda a: pltpu.roll(a, shift, 0), whole)
+        return mat_mat(kept_row(scan, level), rolled,
+                       lambda c, sums: [jnp.where(mask, b, a) for a, b in zip(whole[c], sums)])
+
     def get_mat(ref, *at):
         return [[ref[(*at, c, e)] for e in range(N)] for c in range(N)]
 
@@ -195,17 +222,13 @@
     put_mat(fw, first, 0)
 
     def fw_step(j, carry):
-        carry = mat_mat(mat_map(lambda a: -a, mat_rows(low, j)), carry)
-        put_mat(fw, carry, j)
-        return carry
+        return mat_mat(block_row(low, j), carry, keep(fw, j, sign=-1))
 
     last_f = lax.fori_loop(1, J, fw_step, first)
     steps = (1, 2, 4)
     whole = last_f
     for level, s in enumerate(steps):
-        put_mat(scan_f, mat_map(lambda a: jnp.where(chunk >= s, a, 0.0), whole), level)
-        moved = mat_mat(whole, mat_map(lambda a: pltpu.roll(a, s, 0), whole))
-        whole = mat_map(lambda a, b: jnp.where(chunk >= s, b, a), whole, moved)
+        whole = double(scan_f, level, whole, s, chunk >= s)
     send_map(0, whole, K - 1)
     before = mat_map(lambda a: pltpu.roll(a, 1, 0), whole)
     before = [[jnp.where(chunk >= 1, before[c][e], 1.0 if c == e else 0.0) for e in range(N)] for c in range(N)]
@@ -217,36 +240,33 @@
 
     def bw_step(i, carry):
         j = J - 2 - i
-        carry = mat_mat(mat_map(lambda a: -a, mat_rows(upp, j)), carry)
-        put_mat(bw, carry, j)
-        return carry
+        return mat_mat(block_row(upp, j), carry, keep(bw, j, sign=-1))
 
     def gw_step(i, carry):
         j = J - 2 - i
-        moved = mat_mat(mat_rows(upp, j), carry)
-        carry = mat_map(lambda a, b: a - b, get_mat(fw, j), moved)
-        put_mat(gw, carry, j)
-        return carry
+
+        def finish(c, sums):
+            return keep(gw, j)(c, [fw[j, c, e] - sums[e] for e in range(N)])
+
+        return mat_mat(block_row(upp, j), carry, finish)
 
     first_b = lax.fori_loop(0, J - 1, bw_step, start_b)
-    first_g = lax.fori_loop(0, J - 1, gw_step, last_f)
-
-    seen = mat_mat(first_g, before)
-    put_mat(excl, seen, 1)
+    lax.fori_loop(0, J - 1, gw_step, last_f)
+
+    mat_mat(kept_row(gw, 0), get_mat(excl, 0), keep(excl, 1))
 
     whole = first_b
     for level, s in enumerate(steps):
-        put_mat(scan_b, mat_map(lambda a: jnp.where(chunk < K - s, a, 0.0), whole), level)
-        moved = mat_mat(whole, mat_map(lambda a: pltpu.roll(a, K - s, 0), whole))
-        whole = mat_map(lambda a, b: jnp.where(chunk < K - s, b, a), whole, moved)
+        whole = double(scan_b, level, whole, K - s, chunk < K - s)
     send_map(1, whole, 0)
     after = mat_map(lambda a: pltpu.roll(a, K - 1, 0), whole)
     after = [[jnp.where(chunk < K - 1, after[c][e], 1.0 if c == e else 0.0) for e in range(N)] for c in range(N)]
     put_mat(excl, after, 2)
     seen = get_mat(excl, 1)
     for level, s in enumerate(steps):
-        moved = mat_mat(get_mat(scan_b, level), mat_map(lambda a: pltpu.roll(a, K - s, 0), seen))
-        seen = mat_map(jnp.add, seen, moved)
+        rolled = mat_map(lambda a: pltpu.roll(a, K - s, 0), seen)
+        seen = mat_mat(kept_row(scan_b, level), rolled,
+                       lambda c, sums, seen=seen: vec_add(seen[c], sums))
     send_map(2, seen, 0)
     put_mat(excl, mat_map(lambda a: jnp.where(chunk < K - 1, pltpu.roll(a, K - 1, 0), 0.0), seen), 1)
 

time: 22.9 us -> 22.9 us (level)
  no operation moved by 1% of the time
where the time goes in v5:
time: 22.9 us; the launch traced here: 22.8 us
  Pallas kernels  22.1 us (97%)
  local copies, waits for them, and re-layouts  0.65 us (3%)
    pallas_call x1, Pallas kernels, per_device(): pl.pallas_call(functools.partial(kernel, sizes, J), out_shape=pltpu.VMEM(...  22.1 us
    unnamed x1, local copies, waits for them, and re-layouts  0.65 us

profile of v5, /device:TPU:0, one launch (start us, length us, event | category | flops | bytes accessed | tf_op | source)
XLA Modules:
  0.0 22.8 jit_solution(6544195705272558140)
XLA Ops:
  0.0 22.1 %shard_map.82 = f32[240,128]{1,0:T(8,128)S(1)} custom-call(f32[240,128]{1,0:T(8,128)} %bitcast.14, f32[240,128]{1,0:T(8,128)} %bitcast.15, f32[1200,128]{1,0:T(8,128)} %bitcast.11, f32[1200,128]{1,0:T(8,128)} %bitcast.12, f32[1200,128]{1,0:T(8,128)} %bitcast.13, f32[4800,128]{1,0:T(8,128)} %bitcast.10, s32[48,128]{1,0:T(8,128)} %bitcast.16, s32[48,128]{1,0:T(8,128)} %bitcast.17), custom_call_target="tpu_custom_call" | custom-call | flops 12000000 | bytes 5000000 | tf_op jit(solution)/shard_map/pallas_call | solution.py:487
  22.1 0.7 %copy.12 = f32[48,5,1,128]{3,2,1,0:T(1,128)} copy(f32[48,5,1,128]{3,2,1,0:T(1,128)S(1)} %bitcast.9) | data formatting | bytes 245760
